TPU v7x, 256 devices: a whole 4x4x8 slice. The times are simulated.
256 devices in a mesh: prow: 16 (over y, x), pcol: 16 (over z, core).
Axes of the slice: x: 4, y: 4, z: 8, core: 2. Of those that a mesh axis runs over, the one named last changes fastest.
Arguments:
- matrix: float32 [5, 16, 256, 5, 16, 256], P(None, 'prow', None, None, 'pcol')
Outputs:
- factored: float32 [5, 16, 256, 5, 16, 256], P(None, 'prow', None, None, 'pcol')
All inputs are finite; a program needn't handle non-finite values.
Results may differ from a plain program's by a relative error of at most 0.0003.
Values sent between devices are 32-bit elements; how exact they have to be, the bound alone decides.
A program may use at most 128 MiB of HBM per device.

v0:
```python
import jax
import jax.numpy as jnp
from jax import lax
from jax.sharding import PartitionSpec as P


def broadcast(value, axis, source):
    kept = jnp.where(lax.axis_index(axis) == source, value, 0).astype(value.dtype)
    return lax.psum(kept, axis)


def panel_solve(factor, tiles, grid_row):
    count, width = (tiles.shape[0], tiles.shape[1])
    solved = lax.linalg.triangular_solve(
        factor, tiles.reshape(count * width, width), left_side=False, lower=True, transpose_a=True
    )
    solved = solved.reshape(count, width, width)
    return solved.at[0].set(jnp.where(grid_row == 0, factor, solved[0]))


def per_device(matrix):
    grid_row = lax.axis_index("prow")
    grid_col = lax.axis_index("pcol")
    n_row = lax.axis_size("prow")
    n_col = lax.axis_size("pcol")
    local = matrix[:, 0, :, :, 0, :]
    tile_rows, width, tile_cols = (local.shape[0], local.shape[1], local.shape[2])
    column = local[:, :, 0, :]
    leading = broadcast(local[0, :, 0, :], "prow", 0)
    factor = jnp.linalg.cholesky(leading)
    solved = panel_solve(factor, column, grid_row)
    row_tiles = broadcast(solved, "pcol", 0)
    every = lax.all_gather(row_tiles[:, None], "prow", axis=1, tiled=True)
    col_tiles = lax.dynamic_index_in_dim(every, grid_col, 1, keepdims=False)
    product = jnp.einsum("kab,cdb->kacd", row_tiles, col_tiles, precision=lax.Precision.HIGHEST)
    updated = local - product
    row_global = jnp.arange(tile_rows, dtype=jnp.int32) * n_row + grid_row
    col_global = jnp.arange(tile_cols, dtype=jnp.int32) * n_col + grid_col
    lower = (row_global[:, None] >= col_global[None, :])[:, None, :, None]
    result = jnp.where(lower, updated, jnp.zeros_like(updated))
    first = (col_global == 0)[None, None, :, None]
    result = jnp.where(first, row_tiles[:, :, None, :], result)
    return result[:, None, :, :, None, :]


def solution(mesh):
    return jax.shard_map(
        per_device,
        mesh=mesh,
        in_specs=(P(None, "prow", None, None, "pcol", None),),
        out_specs=P(None, "prow", None, None, "pcol", None),
        check_vma=False,
    )
```

profile of v0, /device:TPU:128, one launch (start us, length us, event | category | flops | bytes accessed | tf_op | source)
XLA Modules:
  0.0 468.0 jit_solution(5706989088490152155)
XLA Ops:
  6.5 0.0 all-reduce.4.cloned.1.call-start
  6.5 14.1 %copy.10 = f32[5,1,256,5,1,256]{2,5,3,0,4,1:T(8,128)} copy(f32[5,1,256,5,1,256]{5,4,3,2,1,0:T(1,128)} %param.3) | data formatting | bytes 13107200 | tf_op args[0]
  20.7 1.7 fusion.9
  22.3 0.0 all-reduce.4.cloned.1.call-update
  22.4 0.0 all-reduce.6.cloned.1.call-start
  22.4 1.4 slice.87
  23.8 0.4 copy.12
  24.3 94.1 %all-reduce.4.cloned.1.call-done = f32[256,256]{0,1:T(8,128)} async-done(((f32[256,256]{0,1:T(8,128)}), f32[256,256]{0,1:T(8,128)}) %all-reduce.4.cloned.1.call-update) | async-done | bytes 262160 | tf_op jit(solution)/shard_map/psum | solution.py:9
  118.4 1.1 copy.11
  119.5 1.0 fusion.10
  120.5 11.7 %cholesky.49 = f32[128,128]{1,0:T(8,128)S(1)} custom-call(f32[128,128]{1,0:T(8,128)S(1)} %cholesky.115), custom_call_target="Cholesky" | custom-call | tf_op jit(solution)/shard_map/jit(cholesky)/cholesky | solution.py:30
  132.2 9.8 %custom-call.14 = f32[1,128,128]{1,2,0:T(8,128)S(1)} custom-call(f32[1,128,128]{2,1,0:T(8,128)S(1)} %get-tuple-element.38), custom_call_target="InvertDiagBlocksLowerTriangular" | custom-call | tf_op jit(solution)/shard_map/jit(cholesky)/cholesky | solution.py:30
  142.0 0.2 constant_dynamic-update-slice_fusion
  142.3 0.3 convolution_subtract_fusion.1
  142.5 11.7 %cholesky.103 = f32[128,128]{1,0:T(8,128)S(1)} custom-call(f32[128,128]{1,0:T(8,128)S(1)} %convolution_subtract_fusion.1), custom_call_target="Cholesky" | custom-call | tf_op jit(solution)/shard_map/jit(cholesky)/cholesky | solution.py:30
  154.3 0.7 compare_reduce_fusion
  156.3 0.1 triangular_solve.59
  156.4 4.2 while.2
  156.5 0.7 fusion.26
  157.2 1.3 bitcast_dynamic-update-slice_fusion.2
  158.5 0.7 fusion.26
  159.2 1.3 bitcast_dynamic-update-slice_fusion.2
  160.6 19.7 %custom-call.15 = f32[2,128,128]{1,2,0:T(8,128)S(1)} custom-call(f32[2,128,128]{2,1,0:T(8,128)S(1)} %get-tuple-element.24), custom_call_target="InvertDiagBlocksLowerTriangular" | custom-call | tf_op jit(solution)/shard_map/triangular_solve | solution.py:14
  180.2 0.8 fusion.3
  181.0 1.2 convolution_subtract_fusion
  182.2 0.2 copy.13
  182.4 0.7 fusion.12
  183.1 0.1 pad_maximum_fusion
  183.3 1.2 broadcast_select_fusion
  184.4 0.0 all-reduce.6.cloned.1.call-update
  184.5 0.0 all-gather.3.cloned.1.call-start
  184.5 111.0 %all-reduce.6.cloned.1.call-done = f32[5,256,256]{2,1,0:T(8,128)} async-done(((f32[5,256,256]{2,1,0:T(8,128)}), f32[5,256,256]{2,1,0:T(8,128)}) %all-reduce.6.cloned.1.call-update) | async-done | bytes 1310736 | tf_op jit(solution)/shard_map/psum | solution.py:9
  295.6 0.0 copy-start
  295.6 0.0 all-gather.3.cloned.1.call-update
  295.6 0.1 broadcast_compare_fusion
  295.7 1.2 copy-done
  296.9 0.4 copy.15
  297.3 140.1 %all-gather.3.cloned.1.call-done = f32[5,4096,256]{2,1,0:T(8,128)} async-done(((f32[5,256,256]{2,1,0:T(8,128)}), f32[5,4096,256]{2,1,0:T(8,128)}) %all-gather.3.cloned.1.call-update) | async-done | bytes 20971536 | tf_op jit(solution)/shard_map/all_gather | solution.py:33
  437.4 9.9 %select_bitcast_fusion = f32[5,1,256,5,1,256]{2,5,3,0,4,1:T(8,128)} fusion(f32[5,256,256]{1,2,0:T(8,128)S(1)} %copy.15, pred[5]{0:T(512)(128)(4,1)S(1)} %broadcast_compare_fusion.1, pred[5,5]{1,0:T(8,128)(4,1)S(1)} %broadcast_compare_fusion, f32[5,256,256]{2,1,0:T(8,128)S(1)} %copy-done, f32[5,16,256,256]{3,2,1,0:T(8,128)} %bitcast.63, s32[]{:T(128)S(6)} %select_n.51, ...), kind=kOutput, calls=%fused_computation.2 | convolution fusion | flops 5038080000 | bytes 17039394 | tf_op jit(solution)/shard_map/kab,cdb->kacd/dot_general | solution.py:35
  447.2 14.2 %copy.18 = f32[5,1,256,5,1,256]{5,4,3,2,1,0:T(1,128)} copy(f32[5,1,256,5,1,256]{2,5,3,0,4,1:T(8,128)} %select_bitcast_fusion) | data formatting | bytes 13107200 | tf_op jit(solution)/shard_map/broadcast_in_dim | solution.py:43
  (13 shorter events, 0.2 us)
Async XLA Ops:
  6.5 111.8 %all-reduce.4.cloned.1.call-start = ((), (), s32[]{:S(2)}) async-start(), calls=%async_computation | async-start | bytes 524288 | tf_op jit(solution)/shard_map/psum | solution.py:9
  22.4 273.2 %all-reduce.6.cloned.1.call-start = ((), (), s32[]{:S(2)}) async-start(), calls=%async_computation.1 | async-start | bytes 2621440 | tf_op jit(solution)/shard_map/psum | solution.py:9
  184.5 252.9 %all-gather.3.cloned.1.call-start = ((), (), s32[]{:S(2)}) async-start(), calls=%async_computation.2 | async-start | bytes 22282240 | tf_op jit(solution)/shard_map/all_gather | solution.py:33
  295.6 1.3 copy-start
Sparse Core Ops, SparseCore 0:
  22.5 95.8 all-reduce.3
  184.6 110.9 all-reduce.5
  298.3 139.0 all-gather.2
where the time goes:
time: 471 us; the launch traced here: 468 us
  waiting for transfers between devices  345 us (73%)
  other arithmetic  57.8 us (12%)
  local copies, waits for them, and re-layouts  37.2 us (8%)
  between operations  14.5 us (3%)
  matrix products  13 us (3%)
    psum x2, waiting for transfers between devices, broadcast(): return lax.psum(kept, axis)  205 us
    all_gather x1, waiting for transfers between devices, per_device(): every = lax.all_gather(row_tiles[:, None], 'prow', axis=1, tiled=True)  140 us
    another operation x6, other arithmetic, per_device(): factor = jnp.linalg.cholesky(leading)  34 us
    another operation x4, other arithmetic, panel_solve(): lax.linalg.triangular_solve(factor, tiles.reshape(count * width, width),...  19.8 us
    unnamed x3, local copies, waits for them, and re-layouts  15.3 us
    broadcast_in_dim x1, local copies, waits for them, and re-layouts, per_device(): return result[:, None, :, :, None, :]  14.2 us
    dot_general x1, matrix products, per_device(): jnp.einsum('kab,cdb->kacd', row_tiles, col_tiles, precision=lax.Precision...  9.87 us
  transfers between devices with their start and end apart: 3, of which 3 were waited for; matrix products, arithmetic and copies ran while one was open for 0% of the time, Pallas kernels for 0%

commit v1 on v0

v1 whole, which is shorter than its diff:
```python
import functools

import jax
import jax.numpy as jnp
from jax import lax
from jax.experimental import pallas as pl
from jax.experimental.pallas import tpu as pltpu
from jax.sharding import PartitionSpec as P

MESH = pl.DeviceIdType.MESH
HI = lax.Precision.HIGHEST
NB, PB, MB = 256, 64, 8
T = 5
ROWS = 64
PER = NB // ROWS
SL = 16


def micro(w_ref, r0, pend):
    lane = lax.broadcasted_iota(jnp.int32, (MB, NB), 1)
    sub = lax.broadcasted_iota(jnp.int32, (MB, NB), 0)
    sub1 = lax.broadcasted_iota(jnp.int32, (MB, 128), 0)
    own = (lane >= r0) & (lane < r0 + MB)
    blk = w_ref[r0:r0 + MB, :]
    d = blk[:, r0:r0 + MB]
    rep = {(i, j): jnp.broadcast_to(d[i:i + 1, j:j + 1], (MB, 128)) for i in range(MB) for j in range(i + 1)}
    low, inv = {}, {}
    a = dict(rep)
    rs = []
    for j in range(MB):
        r = lax.rsqrt(a[j, j])
        rs.append(r)
        for i in range(j + 1, MB):
            low[i, j] = a[i, j] * r
        for k in range(j + 1, MB):
            for i in range(k, MB):
                a[i, k] = a[i, k] - low[i, j] * low[k, j]
    for j in range(MB):
        inv[j, j] = rs[j]
        for i in range(j + 1, MB):
            t = low[i, j] * inv[j, j]
            for k in range(j + 1, i):
                t = t + low[i, k] * inv[k, j]
            inv[i, j] = -t * rs[i]
    ainv = {}
    for i in range(MB):
        for j in range(i + 1):
            t = inv[i, i] * inv[i, j]
            for k in range(i + 1, MB):
                t = t + inv[k, i] * inv[k, j]
            ainv[i, j] = ainv[j, i] = t
    aug = []
    for j in range(MB):
        row = jnp.broadcast_to(w_ref[r0 + j:r0 + j + 1, :], (MB, NB))
        aug.append(jnp.where(own, jnp.where(lane == r0 + j, 1.0, 0.0), row))
    def mix(coef, lower):
        out = None
        for j in range(MB):
            col = jnp.zeros((MB, 128), jnp.float32)
            for i in range(j if lower else 0, MB):
                col = jnp.where(sub1 == i, coef[i, j], col)
            term = jnp.concatenate([col, col], axis=1) * aug[j]
            out = term if out is None else out + term
        return out
    z = mix(ainv, False)
    if pend > r0 + MB:
        rows = w_ref[r0 + MB:pend, :]
        n = pend - r0 - MB
        lane_n = lax.broadcasted_iota(jnp.int32, (n, NB), 1)
        acc = jnp.where((lane_n >= r0) & (lane_n < r0 + MB), 0.0, rows)
        for j in range(MB):
            acc = acc - rows[:, r0 + j:r0 + j + 1] * z[j:j + 1, :]
        w_ref[r0 + MB:pend, :] = acc
    w_ref[r0:r0 + MB, :] = mix(inv, True)

def panel(w_ref, kb):
    p0 = kb * PB
    for m in range(PB // MB):
        micro(w_ref, p0 + m * MB, p0 + PB)
    if p0 + PB < NB:
        r = w_ref[p0:p0 + PB, :]
        n = NB - p0 - PB
        lane_r = lax.broadcasted_iota(jnp.int32, (PB, NB), 1)
        sub_r = lax.broadcasted_iota(jnp.int32, (PB, NB), 0) + p0
        solved = jnp.where((lane_r > sub_r) & (lane_r < p0 + PB), 0.0, r)
        rest = w_ref[p0 + PB:NB, :]
        lane_n = lax.broadcasted_iota(jnp.int32, (n, NB), 1)
        rest = jnp.where((lane_n >= p0) & (lane_n < p0 + PB), 0.0, rest)
        up = lax.dot_general(r[:, p0 + PB:NB], solved, (((0,), (0,)), ((), ())), precision=HI, preferred_element_type=jnp.float32)
        w_ref[p0 + PB:NB, :] = rest - up

def inv_rows(w_ref, kb):
    p0 = kb * PB
    x = w_ref[p0:p0 + PB, :]
    lane = lax.broadcasted_iota(jnp.int32, (PB, NB), 1)
    sub = lax.broadcasted_iota(jnp.int32, (PB, NB), 0) + p0
    return jnp.where(lane <= sub, x, 0.0)


def gather_kernel(a_ref, r_ref, c_ref, i_ref, a_v, w_ref, inv_v, load_sem, send_sem, ysend_sem, csend_sem, r_sem, i_sem, s_sem, g_sem):
    p, q = lax.axis_index("prow"), lax.axis_index("pcol")
    x, y, z, c = lax.rem(p, 4), p // 4, q // 2, lax.rem(q, 2)
    source = q == 0
    owner = jnp.logical_and(p == 0, source)
    bar = pltpu.get_barrier_semaphore()

    def greet(row, col):
        pl.semaphore_signal(bar, 1, device_id=(row, col), device_id_type=MESH)

    def remote(ref, send, recv, row, col):
        return pltpu.make_async_remote_copy(src_ref=ref, dst_ref=ref, send_sem=send, recv_sem=recv, device_id=(row, col), device_id_type=MESH)

    def wait(ref, sem):
        pltpu.make_async_copy(ref, ref, sem).wait()

    def r_chunk(n):
        return r_ref.at[n // PER, pl.ds((n % PER) * ROWS, ROWS), :]

    def i_chunk(m):
        return i_ref.at[pl.ds(m * ROWS, ROWS), :]

    @pl.loop(1, 16)
    def _(d):
        greet(lax.rem(p + d, 16), q)

    @pl.when(jnp.logical_not(owner))
    def _():
        greet(q, 0)

    for kid, parents in ((1, (2,)), (2, (0,)), (3, (2,)), (4, (3, 5)), (5, (6,)), (6, (0,)), (7, (6,))):
        @pl.when(jnp.logical_and(c == 0, z == kid))
        def _(parents=parents):
            for parent in parents:
                greet(p, 2 * parent)

    @pl.when(c == 1)
    def _():
        greet(p, q - 1)

    @pl.when(jnp.logical_and(source, y != 0))
    def _():
        greet(x, 0)

    @pl.when(jnp.logical_and(source, jnp.logical_and(y == 0, x != 0)))
    def _():
        greet(0, 0)

    one = lambda cond: jnp.where(cond, 1, 0)
    near = one(c == 0)
    kids = near + 2 * near * (one(z == 0) + one(z == 2) + one(z == 6)) + near * (one(z == 3) + one(z == 5))
    expect = 15 + one(source) * (16 - one(owner)) + kids + 3 * one(jnp.logical_and(source, y == 0)) + 3 * one(owner)

    def greeted():
        pl.semaphore_wait(bar, expect)

    def pass_on(ref, recv, kids):
        for slot, kid in enumerate(kids):
            remote(ref, send_sem.at[slot], recv, p, 2 * kid).start()
        remote(ref, send_sem.at[2], recv, p, q + 1).start()

    def scatter(t):
        @pl.loop(0, 16)
        def _(s):
            part = pl.ds(pl.multiple_of(s * SL, SL), SL)

            @pl.when(jnp.logical_or(s != 0, jnp.logical_not(owner)))
            def _():
                pltpu.make_async_remote_copy(
                    src_ref=r_ref.at[t, part, :], dst_ref=c_ref.at[t, part, :], send_sem=csend_sem.at[0],
                    recv_sem=s_sem.at[t], device_id=(s, p), device_id_type=MESH).start()

            @pl.when(jnp.logical_and(s == 0, owner))
            def _():
                pltpu.make_async_copy(r_ref.at[t, pl.ds(0, SL), :], c_ref.at[t, pl.ds(0, SL), :], s_sem.at[t]).start()

    mine = pl.ds(pl.multiple_of(p * SL, SL), SL)

    def share(t):
        wait(c_ref.at[t, mine, :], s_sem.at[t])

        @pl.loop(1, 16)
        def _(d):
            remote(c_ref.at[t, mine, :], csend_sem.at[1], g_sem.at[t], lax.rem(p + d, 16), q).start()

    def load(t):
        return pltpu.make_async_copy(a_ref.at[t, 0, :, 0, 0, :], r_ref.at[t], load_sem.at[t])

    @pl.when(owner)
    def _():
        first = pltpu.make_async_copy(a_ref.at[0, 0, :, 0, 0, :], a_v, load_sem.at[0])
        first.start()
        for t in range(1, T):
            load(t).start()
        first.wait()
        a = a_v[...]
        w_ref[...] = 0.5 * (a + a.T)
        a_v[...] = w_ref[...]
        kept = pltpu.make_async_copy(a_v, r_ref.at[0], load_sem.at[0])
        kept.start()
        for kb in range(3):
            panel(w_ref, kb)
            inv_v[kb * PB:(kb + 1) * PB, :] = inv_rows(w_ref, kb)
        kept.wait()
        for t in range(1, T):
            load(t).wait()
        greeted()

        def give(m):
            part = pl.ds(m * ROWS, ROWS)
            src = inv_v.at[part, :]
            to = [(1, 0, 0), (2, 0, 1), (3, 0, 2), (4, 0, 3), (8, 0, 4), (12, 0, 5)]
            for row, col, slot in to:
                pltpu.make_async_remote_copy(src_ref=src, dst_ref=i_chunk(m), send_sem=ysend_sem.at[slot], recv_sem=i_sem.at[m], device_id=(row, col), device_id_type=MESH).start()
            for col, slot in ((4, 0), (12, 1), (1, 2)):
                pltpu.make_async_remote_copy(src_ref=src, dst_ref=i_chunk(m), send_sem=send_sem.at[slot], recv_sem=i_sem.at[m], device_id=(0, col), device_id_type=MESH).start()
            pltpu.make_async_copy(src, i_chunk(m), i_sem.at[m]).start()

        for m in range(3):
            give(m)
        for t in range(T):
            for n in range(PER * t, PER * t + PER):
                pass_on(r_chunk(n), r_sem.at[n], (2, 6))
            scatter(t)
        panel(w_ref, 3)
        inv_v[3 * PB:4 * PB, :] = inv_rows(w_ref, 3)
        give(3)
        for t in range(T):
            share(t)
        for m in range(4):
            wait(i_chunk(m), i_sem.at[m])

    @pl.when(jnp.logical_and(source, jnp.logical_not(owner)))
    def _():
        for t in range(T):
            load(t).start()
        for t in range(T):
            load(t).wait()
        greeted()
        for t in range(T):
            for n in range(PER * t, PER * t + PER):
                pass_on(r_chunk(n), r_sem.at[n], (2, 6))
            scatter(t)
        for m in range(4):
            wait(i_chunk(m), i_sem.at[m])

            @pl.when(y == 0)
            def _():
                for k in range(1, 4):
                    remote(i_chunk(m), ysend_sem.at[k - 1], i_sem.at[m], 4 * k + x, 0).start()
            pass_on(i_chunk(m), i_sem.at[m], (2, 6))
        for t in range(T):
            share(t)

    @pl.when(q != 0)
    def _():
        greeted()

    def relay(ref, sem, n):
        wait(ref, sem)

        @pl.when(z == 2)
        def _():
            for slot, kid in enumerate((1, 3)):
                remote(ref, send_sem.at[slot], sem, p, 2 * kid).start()

        @pl.when(z == 6)
        def _():
            for slot, kid in enumerate((5, 7)):
                remote(ref, send_sem.at[slot], sem, p, 2 * kid).start()

        @pl.when(z == (3 if n % 2 == 0 else 5))
        def _():
            remote(ref, send_sem.at[0], sem, p, 8).start()
        remote(ref, send_sem.at[2], sem, p, q + 1).start()

    @pl.when(jnp.logical_and(c == 0, z != 0))
    def _():
        for t in range(T):
            for n in range(PER * t, PER * t + PER):
                relay(r_chunk(n), r_sem.at[n], n)
            share(t)
        for m in range(4):
            relay(i_chunk(m), i_sem.at[m], m)

    @pl.when(c == 1)
    def _():
        for t in range(T):
            share(t)
        for n in range(T * PER):
            wait(r_chunk(n), r_sem.at[n])
        for m in range(4):
            wait(i_chunk(m), i_sem.at[m])

    for t in range(T):
        wait(c_ref.at[t, pl.ds(0, NB - SL), :], g_sem.at[t])
    wait(c_ref.at[:, pl.ds(0, NB - SL), :], csend_sem.at[1])

    @pl.when(owner)
    def _():
        wait(c_ref.at[:, pl.ds(0, NB - SL), :], csend_sem.at[0])

    @pl.when(jnp.logical_and(source, jnp.logical_not(owner)))
    def _():
        wait(c_ref, csend_sem.at[0])

    @pl.when(jnp.logical_and(source, y == 0))
    def _():
        for k in range(3):
            wait(i_ref, ysend_sem.at[k])

    @pl.when(owner)
    def _():
        for k in range(3, 6):
            wait(i_ref, ysend_sem.at[k])

    def sent(slot):
        wait(r_ref, send_sem.at[slot])
        wait(i_ref, send_sem.at[slot])

    @pl.when(c == 0)
    def _():
        sent(2)

    @pl.when(jnp.logical_and(c == 0, jnp.logical_or(z == 0, jnp.logical_or(z == 2, z == 6))))
    def _():
        sent(0)
        sent(1)

    @pl.when(jnp.logical_and(c == 0, jnp.logical_or(z == 3, z == 5)))
    def _():
        wait(r_ref.at[:, pl.ds(0, NB // 2), :], send_sem.at[0])
        wait(i_ref.at[pl.ds(0, NB // 2), :], send_sem.at[0])


def gather(matrix):
    tiles = jax.ShapeDtypeStruct((T, NB, NB), jnp.float32)
    square = jax.ShapeDtypeStruct((NB, NB), jnp.float32)
    dma = pltpu.SemaphoreType.DMA
    return pl.pallas_call(
        gather_kernel,
        out_shape=(tiles, tiles, square),
        in_specs=[pl.BlockSpec(memory_space=pltpu.HBM)],
        out_specs=[pl.BlockSpec(memory_space=pl.ANY)] * 3,
        scratch_shapes=[
            pltpu.VMEM((NB, NB), jnp.float32), pltpu.VMEM((NB, NB), jnp.float32), pltpu.VMEM((NB, NB), jnp.float32),
            dma((T,)), dma((3,)), dma((6,)), dma((2,)), dma((T * PER,)), dma((4,)), dma((T,)), dma((T,)),
        ],
        compiler_params=pltpu.CompilerParams(collective_id=0, has_side_effects=True, vmem_limit_bytes=16 * 2**20),
        name="gather",
    )(matrix)


def split(v):
    high = v.astype(jnp.bfloat16)
    return high, (v - high.astype(jnp.float32)).astype(jnp.bfloat16)


def times(left, right):
    dims = (((1,), (1,)), ((), ()))
    dot = functools.partial(lax.dot_general, dimension_numbers=dims, preferred_element_type=jnp.float32)
    return dot(left[0], right[0]) + (dot(left[0], right[1]) + dot(left[1], right[0]))


PAIRS = [(k, j) for k in range(T) for j in range(k + 1)]


def update_kernel(a_ref, r_ref, c_ref, i_ref, o_ref, a_v, z_v, x_v, rh, rl, ch, cl, load_sem, store_sem, zero_sem):
    p, q = lax.axis_index("prow"), lax.axis_index("pcol")

    def load(n):
        k, j = PAIRS[n]
        return pltpu.make_async_copy(a_ref.at[k, 0, :, j, 0, :], a_v.at[n], load_sem.at[n])

    def store(n):
        k, j = PAIRS[n]
        return pltpu.make_async_copy(a_v.at[n], o_ref.at[k, 0, :, j, 0, :], store_sem.at[n])

    for n in range(len(PAIRS)):
        load(n).start()
    z_v[...] = jnp.zeros_like(z_v)
    blank = [pltpu.make_async_copy(z_v, o_ref.at[k, 0, :, j, 0, :], zero_sem) for k in range(T) for j in range(k + 1, T)]
    for copy in blank:
        copy.start()
    inv = split(i_ref[...])
    for k in range(T):
        v = times(split(r_ref[k]), inv)
        x_v[k] = v
        rh[k], rl[k] = split(v)
        ch[k], cl[k] = split(times(split(c_ref[k]), inv))

    @pl.when(jnp.logical_and(p == 0, q == 0))
    def _():
        row = lax.broadcasted_iota(jnp.int32, (NB, NB), 0)
        col = lax.broadcasted_iota(jnp.int32, (NB, NB), 1)
        x_v[0] = jnp.where(col <= row, x_v[0], 0.0)

    for n, (k, j) in enumerate(PAIRS):
        load(n).wait()
        v = a_v[n] - times((rh[k], rl[k]), (ch[j], cl[j]))
        if k == j:
            v = jnp.where(p >= q, v, 0.0)
        if j == 0:
            v = jnp.where(q == 0, x_v[k], v)
        a_v[n] = v
        store(n).start()
    for copy in blank:
        copy.wait()
    for n in range(len(PAIRS)):
        store(n).wait()


def update(matrix, r, c, i):
    vmem = pl.BlockSpec(memory_space=pltpu.VMEM)
    half = pltpu.VMEM((T, NB, NB), jnp.bfloat16)
    dma = pltpu.SemaphoreType.DMA
    return pl.pallas_call(
        update_kernel,
        out_shape=jax.ShapeDtypeStruct(matrix.shape, jnp.float32),
        in_specs=[pl.BlockSpec(memory_space=pl.ANY), vmem, vmem, vmem],
        out_specs=pl.BlockSpec(memory_space=pl.ANY),
        scratch_shapes=[
            pltpu.VMEM((len(PAIRS), NB, NB), jnp.float32), pltpu.VMEM((NB, NB), jnp.float32), pltpu.VMEM((T, NB, NB), jnp.float32),
            half, half, half, half, dma((len(PAIRS),)), dma((len(PAIRS),)), dma,
        ],
        compiler_params=pltpu.CompilerParams(vmem_limit_bytes=32 * 2**20),
        name="update",
    )(matrix, r, c, i)


def per_device(matrix):
    r, c, i = gather(matrix)
    return update(matrix, r, c, i)


def solution(mesh):
    spec = P(None, "prow", None, None, "pcol", None)
    return jax.shard_map(per_device, mesh=mesh, in_specs=(spec,), out_specs=spec, check_vma=False)
```

time: 471 us -> 65 us (0.14)
  waiting for transfers between devices: 345 us -> 0 us
  Pallas kernels: 0 us -> 61.5 us
  other arithmetic: 57.8 us -> 0 us
  local copies, waits for them, and re-layouts: 37.2 us -> 2.86 us
  between operations: 14.5 us -> 0.18 us
  matrix products: 13 us -> 0 us
    psum x2 -> x0, waiting for transfers between devices: 205 us -> none  [broadcast(): return lax.psum(kept, axis)]
    all_gather x1 -> x0, waiting for transfers between devices: 140 us -> none  [per_device(): every = lax.all_gather(row_tiles[:, None], 'prow', axis=1, tiled=True)]
    pallas_call x0 -> x2, Pallas kernels: none -> 61.5 us  [the longest x1 50.7 us: gather(): pl.pallas_call(gather_kernel, out_shape=(tiles, tiles, square), in_specs=...]
    another operation x10 -> x0, other arithmetic: 53.8 us -> none  [the longest x6 34 us: per_device(): factor = jnp.linalg.cholesky(leading)]
    broadcast_in_dim x1 -> x0, local copies, waits for them, and re-layouts: 14.2 us -> none  [per_device(): return result[:, None, :, :, None, :]]
    unnamed x3 -> x4, local copies, waits for them, and re-layouts: 15.3 us -> 2.86 us
    dot_general x1 -> x0, matrix products: 9.87 us -> none  [per_device(): jnp.einsum('kab,cdb->kacd', row_tiles, col_tiles, precision=lax.Precision...]
  transfers between devices with their start and end apart: 3 -> 0, of which waited for: 3 -> 0; matrix products, arithmetic and copies ran while one was open for 0% -> 0% of each run, Pallas kernels for 0% -> 0%
where the time goes in v1:
time: 65 us; the launch traced here: 64.5 us
  Pallas kernels  61.5 us (95%)
  local copies, waits for them, and re-layouts  2.86 us (4%)
    pallas_call x1, Pallas kernels, gather(): pl.pallas_call(gather_kernel, out_shape=(tiles, tiles, square), in_specs=...  50.7 us
    pallas_call x1, Pallas kernels, update(): pl.pallas_call(update_kernel, out_shape=jax.ShapeDtypeStruct(matrix.shape...  10.8 us
    unnamed x4, local copies, waits for them, and re-layouts  2.86 us

profile of v1, /device:TPU:128, one launch (start us, length us, event | category | flops | bytes accessed | tf_op | source)
XLA Modules:
  0.0 64.5 jit_solution(816351573656008334)
XLA Ops:
  0.0 0.0 copy-start
  0.0 2.9 %copy-done = f32[5,1,256,5,1,256]{5,4,3,2,1,0:T(1,128)S(1)} copy-done((f32[5,1,256,5,1,256]{5,4,3,2,1,0:T(1,128)S(1)}, f32[5,1,256,5,1,256]{5,4,3,2,1,0:T(1,128)}, u32[]{:S(2)}) %copy-start) | copy-done | bytes 6553624
  2.9 0.0 copy-start.1
  2.9 50.7 %gather.1 = (f32[5,256,256]{2,1,0:T(8,128)S(1)}, f32[5,256,256]{2,1,0:T(8,128)S(1)}, f32[256,256]{1,0:T(8,128)S(1)}) custom-call(f32[5,1,256,5,1,256]{5,4,3,2,1,0:T(1,128)S(1)} %copy-done), custom_call_target="tpu_custom_call" | custom-call | tf_op jit(solution)/shard_map/gather/pallas_call | solution.py:339
  53.5 0.0 copy-done.1
  53.6 10.8 %update.1 = f32[5,1,256,5,1,256]{5,4,3,2,1,0:T(1,128)} custom-call(f32[5,1,256,5,1,256]{5,4,3,2,1,0:T(1,128)S(1)} %copy-done.1, f32[5,256,256]{2,1,0:T(8,128)S(1)} %get-tuple-element.8.r_ref, f32[5,256,256]{2,1,0:T(8,128)S(1)} %get-tuple-element.9.c_ref, f32[256,256]{1,0:T(8,128)S(1)} %get-tuple-element.10.i_ref), custom_call_target="tpu_custom_call" | custom-call | tf_op jit(solution)/shard_map/update/pallas_call | solution.py:416
Async XLA Ops:
  0.0 2.9 %copy-start = (f32[5,1,256,5,1,256]{5,4,3,2,1,0:T(1,128)S(1)}, f32[5,1,256,5,1,256]{5,4,3,2,1,0:T(1,128)}, u32[]{:S(2)}) copy-start(f32[5,1,256,5,1,256]{5,4,3,2,1,0:T(1,128)} %a_ref.3) | copy-start | bytes 19660804
  2.9 50.7 %copy-start.1 = (f32[5,1,256,5,1,256]{5,4,3,2,1,0:T(1,128)S(1)}, f32[5,1,256,5,1,256]{5,4,3,2,1,0:T(1,128)}, u32[]{:S(2)}) copy-start(f32[5,1,256,5,1,256]{5,4,3,2,1,0:T(1,128)} %a_ref.3) | copy-start | bytes 19660804

commit v2 on v1

--- a/solution.py
+++ b/solution.py
@@ -345,7 +345,7 @@
             pltpu.VMEM((NB, NB), jnp.float32), pltpu.VMEM((NB, NB), jnp.float32), pltpu.VMEM((NB, NB), jnp.float32),
             dma((T,)), dma((3,)), dma((6,)), dma((2,)), dma((T * PER,)), dma((4,)), dma((T,)), dma((T,)),
         ],
-        compiler_params=pltpu.CompilerParams(collective_id=0, has_side_effects=True, vmem_limit_bytes=16 * 2**20),
+        compiler_params=pltpu.CompilerParams(collective_id=0, has_side_effects=True, vmem_limit_bytes=50 * 2**20),
         name="gather",
     )(matrix)
 
@@ -355,76 +355,85 @@
     return high, (v - high.astype(jnp.float32)).astype(jnp.bfloat16)
 
 
+def left_parts(v):
+    high, low = split(v)
+    return jnp.concatenate([high, high, low], axis=1)
+
+
+def right_parts(v):
+    high, low = split(v)
+    return jnp.concatenate([high, low, high], axis=1)
+
+
 def times(left, right):
-    dims = (((1,), (1,)), ((), ()))
-    dot = functools.partial(lax.dot_general, dimension_numbers=dims, preferred_element_type=jnp.float32)
-    return dot(left[0], right[0]) + (dot(left[0], right[1]) + dot(left[1], right[0]))
-
-
-PAIRS = [(k, j) for k in range(T) for j in range(k + 1)]
-
-
-def update_kernel(a_ref, r_ref, c_ref, i_ref, o_ref, a_v, z_v, x_v, rh, rl, ch, cl, load_sem, store_sem, zero_sem):
+    return lax.dot_general(left, right, (((1,), (1,)), ((), ())), preferred_element_type=jnp.float32)
+
+
+LANES = 128
+STRIDE = T * NB // LANES
+ROW_LINES = NB * STRIDE
+
+
+def update_kernel(a_ref, r_ref, c_ref, i_ref, o_ref, o_v, x_v, inv3, r3, c3, store_sem):
     p, q = lax.axis_index("prow"), lax.axis_index("pcol")
 
-    def load(n):
-        k, j = PAIRS[n]
-        return pltpu.make_async_copy(a_ref.at[k, 0, :, j, 0, :], a_v.at[n], load_sem.at[n])
-
-    def store(n):
-        k, j = PAIRS[n]
-        return pltpu.make_async_copy(a_v.at[n], o_ref.at[k, 0, :, j, 0, :], store_sem.at[n])
-
-    for n in range(len(PAIRS)):
-        load(n).start()
-    z_v[...] = jnp.zeros_like(z_v)
-    blank = [pltpu.make_async_copy(z_v, o_ref.at[k, 0, :, j, 0, :], zero_sem) for k in range(T) for j in range(k + 1, T)]
-    for copy in blank:
-        copy.start()
-    inv = split(i_ref[...])
+    def lines(k, j, h):
+        return pl.ds(k * ROW_LINES + j * (NB // LANES) + h, NB, stride=STRIDE)
+
+    def put(k, j, v):
+        for h in range(NB // LANES):
+            o_v[lines(k, j, h), :] = v[:, h * LANES:(h + 1) * LANES]
+
+    def store(k):
+        part = pl.ds(k * ROW_LINES, ROW_LINES)
+        return pltpu.make_async_copy(o_v.at[part, :], o_ref.at[part, :], store_sem.at[k])
+
+    inv3[...] = right_parts(i_ref[...])
     for k in range(T):
-        v = times(split(r_ref[k]), inv)
-        x_v[k] = v
-        rh[k], rl[k] = split(v)
-        ch[k], cl[k] = split(times(split(c_ref[k]), inv))
-
-    @pl.when(jnp.logical_and(p == 0, q == 0))
-    def _():
-        row = lax.broadcasted_iota(jnp.int32, (NB, NB), 0)
-        col = lax.broadcasted_iota(jnp.int32, (NB, NB), 1)
-        x_v[0] = jnp.where(col <= row, x_v[0], 0.0)
-
-    for n, (k, j) in enumerate(PAIRS):
-        load(n).wait()
-        v = a_v[n] - times((rh[k], rl[k]), (ch[j], cl[j]))
-        if k == j:
-            v = jnp.where(p >= q, v, 0.0)
-        if j == 0:
-            v = jnp.where(q == 0, x_v[k], v)
-        a_v[n] = v
-        store(n).start()
-    for copy in blank:
-        copy.wait()
-    for n in range(len(PAIRS)):
-        store(n).wait()
+        c3[k] = right_parts(times(left_parts(c_ref[k]), inv3[...]))
+    for k in range(T):
+        v = times(left_parts(r_ref[k]), inv3[...])
+        r3[k] = left_parts(v)
+        x_v[...] = v
+        if k == 0:
+            @pl.when(jnp.logical_and(p == 0, q == 0))
+            def _():
+                row = lax.broadcasted_iota(jnp.int32, (NB, NB), 0)
+                col = lax.broadcasted_iota(jnp.int32, (NB, NB), 1)
+                x_v[...] = jnp.where(col <= row, x_v[...], 0.0)
+        for j in range(T):
+            if j > k:
+                put(k, j, jnp.zeros((NB, NB), jnp.float32))
+                continue
+            a = jnp.concatenate([a_ref[lines(k, j, h), :] for h in range(NB // LANES)], axis=1)
+            v = a - times(r3[k], c3[j])
+            if k == j:
+                v = jnp.where(p >= q, v, 0.0)
+            if j == 0:
+                v = jnp.where(q == 0, x_v[...], v)
+            put(k, j, v)
+        store(k).start()
+    for k in range(T):
+        store(k).wait()
 
 
 def update(matrix, r, c, i):
     vmem = pl.BlockSpec(memory_space=pltpu.VMEM)
-    half = pltpu.VMEM((T, NB, NB), jnp.bfloat16)
-    dma = pltpu.SemaphoreType.DMA
-    return pl.pallas_call(
+    flat = (matrix.size // LANES, LANES)
+    thirds = pltpu.VMEM((T, NB, 3 * NB), jnp.bfloat16)
+    out = pl.pallas_call(
         update_kernel,
-        out_shape=jax.ShapeDtypeStruct(matrix.shape, jnp.float32),
-        in_specs=[pl.BlockSpec(memory_space=pl.ANY), vmem, vmem, vmem],
+        out_shape=jax.ShapeDtypeStruct(flat, jnp.float32),
+        in_specs=[vmem, vmem, vmem, vmem],
         out_specs=pl.BlockSpec(memory_space=pl.ANY),
         scratch_shapes=[
-            pltpu.VMEM((len(PAIRS), NB, NB), jnp.float32), pltpu.VMEM((NB, NB), jnp.float32), pltpu.VMEM((T, NB, NB), jnp.float32),
-            half, half, half, half, dma((len(PAIRS),)), dma((len(PAIRS),)), dma,
+            pltpu.VMEM(flat, jnp.float32), pltpu.VMEM((NB, NB), jnp.float32), pltpu.VMEM((NB, 3 * NB), jnp.bfloat16), thirds, thirds,
+            pltpu.SemaphoreType.DMA((T,)),
         ],
         compiler_params=pltpu.CompilerParams(vmem_limit_bytes=32 * 2**20),
         name="update",
-    )(matrix, r, c, i)
+    )(matrix.reshape(flat), r, c, i)
+    return out.reshape(matrix.shape)
 
 
 def per_device(matrix):

time: 65 us -> 56 us (0.86)
  Pallas kernels: 61.5 us -> 55.5 us
  local copies, waits for them, and re-layouts: 2.86 us -> 0.01 us
    pallas_call x1, Pallas kernels: 10.8 us -> 4.73 us  [update(): pl.pallas_call(update_kernel, out_shape=jax.ShapeDtypeStruct(flat, jnp.fl...]
    unnamed x4 -> x2, local copies, waits for them, and re-layouts: 2.86 us -> 0.01 us
where the time goes in v2:
time: 56 us; the launch traced here: 55.5 us
  Pallas kernels  55.5 us (99%)
    pallas_call x1, Pallas kernels, gather(): pl.pallas_call(gather_kernel, out_shape=(tiles, tiles, square), in_specs=...  50.8 us
    pallas_call x1, Pallas kernels, update(): pl.pallas_call(update_kernel, out_shape=jax.ShapeDtypeStruct(flat, jnp.fl...  4.73 us

profile of v2, /device:TPU:128, one launch (start us, length us, event | category | flops | bytes accessed | tf_op | source)
XLA Modules:
  0.0 55.5 jit_solution(6924151101543788730)
XLA Ops:
  0.0 0.0 copy-start
  0.0 50.8 %gather.1 = (f32[5,256,256]{2,1,0:T(8,128)S(1)}, f32[5,256,256]{2,1,0:T(8,128)S(1)}, f32[256,256]{1,0:T(8,128)S(1)}) custom-call(f32[5,1,256,5,1,256]{5,4,3,2,1,0:T(1,128)} %a_ref.1), custom_call_target="tpu_custom_call" | custom-call | tf_op jit(solution)/shard_map/gather/pallas_call | solution.py:339
  50.8 0.0 copy-done
  50.8 4.7 %update.1 = f32[12800,128]{1,0:T(8,128)} custom-call(f32[12800,128]{1,0:T(8,128)S(1)} %bitcast.2, f32[5,256,256]{2,1,0:T(8,128)S(1)} %get-tuple-element.8.r_ref, f32[5,256,256]{2,1,0:T(8,128)S(1)} %get-tuple-element.9.c_ref, f32[256,256]{1,0:T(8,128)S(1)} %get-tuple-element.10.i_ref), custom_call_target="tpu_custom_call" | custom-call | tf_op jit(solution)/shard_map/update/pallas_call | solution.py:424
Async XLA Ops:
  0.0 50.8 %copy-start = (f32[5,1,256,5,1,256]{5,4,3,2,1,0:T(1,128)S(1)}, f32[5,1,256,5,1,256]{5,4,3,2,1,0:T(1,128)}, u32[]{:S(2)}) copy-start(f32[5,1,256,5,1,256]{5,4,3,2,1,0:T(1,128)} %a_ref.1) | copy-start | bytes 19660804

commit v3 on v2

--- a/solution.py
+++ b/solution.py
@@ -97,11 +97,21 @@
     return jnp.where(lane <= sub, x, 0.0)
 
 
-def gather_kernel(a_ref, r_ref, c_ref, i_ref, a_v, w_ref, inv_v, load_sem, send_sem, ysend_sem, csend_sem, r_sem, i_sem, s_sem, g_sem):
+ORDER = (1, 2, 3, 4, 0)
+STEPS = (("r", 0), ("r", 1), ("s", 0), ("r", 2), ("s", 1), ("y", 0), ("r", 3), ("s", 2), ("y", 1), ("r", 4), ("s", 3), ("y", 2), ("s", 4), ("y", 3), ("y", 4), ("i", 0), ("i", 1), ("i", 2), ("i", 3))
+
+
+def gather_kernel(a_ref, r_ref, c_ref, i_ref, a_v, w_ref, inv_v, load_sem, send_sem, ysend_sem, csend_sem, r_sem, i_sem, s_sem, x_sem, g_sem):
     p, q = lax.axis_index("prow"), lax.axis_index("pcol")
     x, y, z, c = lax.rem(p, 4), p // 4, q // 2, lax.rem(q, 2)
+    both = jnp.logical_and
     source = q == 0
-    owner = jnp.logical_and(p == 0, source)
+    owner = both(p == 0, source)
+    plain_source = both(p != 0, source)
+    lead = p == q
+    first, second = c == 0, c == 1
+    spread = both(q == 1, both(y == 0, x != 0))
+    beside_owner = both(q == 1, p == 0)
     bar = pltpu.get_barrier_semaphore()
 
     def greet(row, col):
@@ -119,217 +129,239 @@
     def i_chunk(m):
         return i_ref.at[pl.ds(m * ROWS, ROWS), :]
 
-    @pl.loop(1, 16)
-    def _(d):
-        greet(lax.rem(p + d, 16), q)
-
-    @pl.when(jnp.logical_not(owner))
-    def _():
-        greet(q, 0)
+    for d in range(1, 4):
+        greet(4 * y + lax.rem(x + d, 4), q)
+        greet(4 * lax.rem(y + d, 4) + x, q)
+
+    @pl.when(jnp.logical_not(lead))
+    def _():
+        greet(q, q)
 
     for kid, parents in ((1, (2,)), (2, (0,)), (3, (2,)), (4, (3, 5)), (5, (6,)), (6, (0,)), (7, (6,))):
-        @pl.when(jnp.logical_and(c == 0, z == kid))
+        @pl.when(z == kid)
         def _(parents=parents):
             for parent in parents:
-                greet(p, 2 * parent)
-
-    @pl.when(c == 1)
+                greet(p, 2 * parent + c)
+
+    @pl.when(second)
     def _():
         greet(p, q - 1)
 
-    @pl.when(jnp.logical_and(source, y != 0))
-    def _():
-        greet(x, 0)
-
-    @pl.when(jnp.logical_and(source, jnp.logical_and(y == 0, x != 0)))
-    def _():
-        greet(0, 0)
+    @pl.when(both(first, jnp.logical_not(owner)))
+    def _():
+        greet(p, q + 1)
+
+    @pl.when(q == 1)
+    def _():
+        @pl.when(both(x != 0, y != 0))
+        def _():
+            greet(x, 1)
+
+        @pl.when(jnp.logical_or(x == 0, y == 0))
+        def _():
+            greet(0, 0)
 
     one = lambda cond: jnp.where(cond, 1, 0)
-    near = one(c == 0)
-    kids = near + 2 * near * (one(z == 0) + one(z == 2) + one(z == 6)) + near * (one(z == 3) + one(z == 5))
-    expect = 15 + one(source) * (16 - one(owner)) + kids + 3 * one(jnp.logical_and(source, y == 0)) + 3 * one(owner)
+    along = 2 * (one(z == 0) + one(z == 2) + one(z == 6)) + one(z == 3) + one(z == 5)
+    expect = 6 + 15 * one(lead) + along + 1 - one(beside_owner) + 3 * one(spread) + 7 * one(owner)
 
     def greeted():
         pl.semaphore_wait(bar, expect)
 
-    def pass_on(ref, recv, kids):
-        for slot, kid in enumerate(kids):
-            remote(ref, send_sem.at[slot], recv, p, 2 * kid).start()
-        remote(ref, send_sem.at[2], recv, p, q + 1).start()
+    def pass_z(ref, sem, n):
+        for parent, kids in ((0, (2, 6)), (2, (1, 3)), (6, (5, 7)), (3 if n % 2 == 0 else 5, (4,))):
+            @pl.when(z == parent)
+            def _(kids=kids):
+                for slot, kid in enumerate(kids):
+                    remote(ref, send_sem.at[slot], sem, p, 2 * kid + c).start()
+
+    def send_r(t):
+        for n in range(PER * t, PER * t + PER):
+            pass_z(r_chunk(n), r_sem.at[n], n)
+            remote(r_chunk(n), send_sem.at[2], r_sem.at[n], p, q + 1).start()
+
+    def relay_i(m):
+        wait(i_chunk(m), i_sem.at[m])
+
+        @pl.when(spread)
+        def _():
+            for k in range(1, 4):
+                remote(i_chunk(m), ysend_sem.at[k - 1], i_sem.at[m], 4 * k + x, 1).start()
+        pass_z(i_chunk(m), i_sem.at[m], m)
+
+        @pl.when(jnp.logical_not(beside_owner))
+        def _():
+            remote(i_chunk(m), send_sem.at[2], i_sem.at[m], p, q - 1).start()
+
+    mine = pl.ds(pl.multiple_of(p * SL, SL), SL)
 
     def scatter(t):
-        @pl.loop(0, 16)
-        def _(s):
-            part = pl.ds(pl.multiple_of(s * SL, SL), SL)
-
-            @pl.when(jnp.logical_or(s != 0, jnp.logical_not(owner)))
-            def _():
-                pltpu.make_async_remote_copy(
-                    src_ref=r_ref.at[t, part, :], dst_ref=c_ref.at[t, part, :], send_sem=csend_sem.at[0],
-                    recv_sem=s_sem.at[t], device_id=(s, p), device_id_type=MESH).start()
-
-            @pl.when(jnp.logical_and(s == 0, owner))
-            def _():
-                pltpu.make_async_copy(r_ref.at[t, pl.ds(0, SL), :], c_ref.at[t, pl.ds(0, SL), :], s_sem.at[t]).start()
-
-    mine = pl.ds(pl.multiple_of(p * SL, SL), SL)
+        @pl.loop(1, 16)
+        def _(d):
+            row = lax.rem(p + d, 16)
+            part = pl.ds(pl.multiple_of(row * SL, SL), SL)
+            pltpu.make_async_remote_copy(
+                src_ref=r_ref.at[t, part, :], dst_ref=c_ref.at[t, part, :], send_sem=csend_sem.at[0],
+                recv_sem=s_sem.at[t], device_id=(row, q), device_id_type=MESH).start()
+        pltpu.make_async_copy(r_ref.at[t, mine, :], c_ref.at[t, mine, :], s_sem.at[t]).start()
 
     def share(t):
         wait(c_ref.at[t, mine, :], s_sem.at[t])
-
-        @pl.loop(1, 16)
-        def _(d):
-            remote(c_ref.at[t, mine, :], csend_sem.at[1], g_sem.at[t], lax.rem(p + d, 16), q).start()
+        for d in range(1, 4):
+            remote(c_ref.at[t, mine, :], csend_sem.at[1], x_sem.at[t], 4 * y + lax.rem(x + d, 4), q).start()
+
+    def share_y(t):
+        wait(c_ref.at[t, pl.ds(0, 3 * SL), :], x_sem.at[t])
+        ours = c_ref.at[t, pl.ds(pl.multiple_of(y * 4 * SL, 4 * SL), 4 * SL), :]
+        for d in range(1, 4):
+            remote(ours, csend_sem.at[2], g_sem.at[t], 4 * lax.rem(y + d, 4) + x, q).start()
 
     def load(t):
         return pltpu.make_async_copy(a_ref.at[t, 0, :, 0, 0, :], r_ref.at[t], load_sem.at[t])
 
+    def factor(kb):
+        panel(w_ref, kb)
+        inv_v[kb * PB:(kb + 1) * PB, :] = inv_rows(w_ref, kb)
+
+    def give(m):
+        src = inv_v.at[pl.ds(m * ROWS, ROWS), :]
+        for slot, row in enumerate((1, 2, 3, 4, 8, 12, 0)):
+            pltpu.make_async_remote_copy(src_ref=src, dst_ref=i_chunk(m), send_sem=ysend_sem.at[slot], recv_sem=i_sem.at[m], device_id=(row, 1), device_id_type=MESH).start()
+        pltpu.make_async_copy(src, i_chunk(m), i_sem.at[m]).start()
+
     @pl.when(owner)
     def _():
-        first = pltpu.make_async_copy(a_ref.at[0, 0, :, 0, 0, :], a_v, load_sem.at[0])
-        first.start()
+        lead_tile = pltpu.make_async_copy(a_ref.at[0, 0, :, 0, 0, :], a_v, load_sem.at[0])
+        lead_tile.start()
         for t in range(1, T):
             load(t).start()
-        first.wait()
+        lead_tile.wait()
         a = a_v[...]
         w_ref[...] = 0.5 * (a + a.T)
         a_v[...] = w_ref[...]
         kept = pltpu.make_async_copy(a_v, r_ref.at[0], load_sem.at[0])
         kept.start()
-        for kb in range(3):
-            panel(w_ref, kb)
-            inv_v[kb * PB:(kb + 1) * PB, :] = inv_rows(w_ref, kb)
+        factor(0)
+        factor(1)
         kept.wait()
         for t in range(1, T):
             load(t).wait()
         greeted()
-
-        def give(m):
-            part = pl.ds(m * ROWS, ROWS)
-            src = inv_v.at[part, :]
-            to = [(1, 0, 0), (2, 0, 1), (3, 0, 2), (4, 0, 3), (8, 0, 4), (12, 0, 5)]
-            for row, col, slot in to:
-                pltpu.make_async_remote_copy(src_ref=src, dst_ref=i_chunk(m), send_sem=ysend_sem.at[slot], recv_sem=i_sem.at[m], device_id=(row, col), device_id_type=MESH).start()
-            for col, slot in ((4, 0), (12, 1), (1, 2)):
-                pltpu.make_async_remote_copy(src_ref=src, dst_ref=i_chunk(m), send_sem=send_sem.at[slot], recv_sem=i_sem.at[m], device_id=(0, col), device_id_type=MESH).start()
-            pltpu.make_async_copy(src, i_chunk(m), i_sem.at[m]).start()
-
-        for m in range(3):
-            give(m)
-        for t in range(T):
-            for n in range(PER * t, PER * t + PER):
-                pass_on(r_chunk(n), r_sem.at[n], (2, 6))
+        give(0)
+        give(1)
+        for t in (1, 2):
+            send_r(t)
             scatter(t)
-        panel(w_ref, 3)
-        inv_v[3 * PB:4 * PB, :] = inv_rows(w_ref, 3)
+        factor(2)
+        give(2)
+        send_r(3)
+        scatter(3)
+        factor(3)
         give(3)
-        for t in range(T):
+        for t in (4, 0):
+            send_r(t)
+            scatter(t)
+
+    @pl.when(plain_source)
+    def _():
+        for t in ORDER:
+            load(t).start()
+        greeted()
+        for t in ORDER:
+            load(t).wait()
+            send_r(t)
+
+    @pl.when(source)
+    def _():
+        for n, t in enumerate(ORDER):
             share(t)
+            if n > 0:
+                share_y(ORDER[n - 1])
+        share_y(ORDER[-1])
+
+    @pl.when(q != 0)
+    def _():
+        greeted()
+
+    def take(t):
+        for n in range(PER * t, PER * t + PER):
+            wait(r_chunk(n), r_sem.at[n])
+
+            @pl.when(first)
+            def _(n=n):
+                pass_z(r_chunk(n), r_sem.at[n], n)
+                remote(r_chunk(n), send_sem.at[2], r_sem.at[n], p, q + 1).start()
+
+        @pl.when(lead)
+        def _():
+            scatter(t)
+
+    @pl.when(q != 0)
+    def _():
+        for step in STEPS:
+            kind, n = step
+            if kind == "r":
+                take(ORDER[n])
+            elif kind == "s":
+                share(ORDER[n])
+            elif kind == "y":
+                share_y(ORDER[n])
+            else:
+                pl.when(second)(functools.partial(relay_i, n))
+
+    @pl.when(first)
+    def _():
         for m in range(4):
             wait(i_chunk(m), i_sem.at[m])
-
-    @pl.when(jnp.logical_and(source, jnp.logical_not(owner)))
-    def _():
-        for t in range(T):
-            load(t).start()
-        for t in range(T):
-            load(t).wait()
-        greeted()
-        for t in range(T):
-            for n in range(PER * t, PER * t + PER):
-                pass_on(r_chunk(n), r_sem.at[n], (2, 6))
-            scatter(t)
-        for m in range(4):
-            wait(i_chunk(m), i_sem.at[m])
-
-            @pl.when(y == 0)
-            def _():
-                for k in range(1, 4):
-                    remote(i_chunk(m), ysend_sem.at[k - 1], i_sem.at[m], 4 * k + x, 0).start()
-            pass_on(i_chunk(m), i_sem.at[m], (2, 6))
-        for t in range(T):
-            share(t)
-
-    @pl.when(q != 0)
-    def _():
-        greeted()
-
-    def relay(ref, sem, n):
-        wait(ref, sem)
-
-        @pl.when(z == 2)
-        def _():
-            for slot, kid in enumerate((1, 3)):
-                remote(ref, send_sem.at[slot], sem, p, 2 * kid).start()
-
-        @pl.when(z == 6)
-        def _():
-            for slot, kid in enumerate((5, 7)):
-                remote(ref, send_sem.at[slot], sem, p, 2 * kid).start()
-
-        @pl.when(z == (3 if n % 2 == 0 else 5))
-        def _():
-            remote(ref, send_sem.at[0], sem, p, 8).start()
-        remote(ref, send_sem.at[2], sem, p, q + 1).start()
-
-    @pl.when(jnp.logical_and(c == 0, z != 0))
-    def _():
-        for t in range(T):
-            for n in range(PER * t, PER * t + PER):
-                relay(r_chunk(n), r_sem.at[n], n)
-            share(t)
-        for m in range(4):
-            relay(i_chunk(m), i_sem.at[m], m)
-
-    @pl.when(c == 1)
-    def _():
-        for t in range(T):
-            share(t)
-        for n in range(T * PER):
-            wait(r_chunk(n), r_sem.at[n])
-        for m in range(4):
-            wait(i_chunk(m), i_sem.at[m])
-
-    for t in range(T):
-        wait(c_ref.at[t, pl.ds(0, NB - SL), :], g_sem.at[t])
-    wait(c_ref.at[:, pl.ds(0, NB - SL), :], csend_sem.at[1])
+    for t in ORDER:
+        wait(c_ref.at[t, pl.ds(0, NB - 4 * SL), :], g_sem.at[t])
+    wait(c_ref.at[:, pl.ds(0, 3 * SL), :], csend_sem.at[1])
+    wait(c_ref.at[:, pl.ds(0, NB - 4 * SL), :], csend_sem.at[2])
+
+    @pl.when(lead)
+    def _():
+        wait(c_ref.at[:, pl.ds(0, NB - SL), :], csend_sem.at[0])
 
     @pl.when(owner)
     def _():
-        wait(c_ref.at[:, pl.ds(0, NB - SL), :], csend_sem.at[0])
-
-    @pl.when(jnp.logical_and(source, jnp.logical_not(owner)))
-    def _():
-        wait(c_ref, csend_sem.at[0])
-
-    @pl.when(jnp.logical_and(source, y == 0))
+        for k in range(7):
+            wait(i_ref, ysend_sem.at[k])
+
+    @pl.when(spread)
     def _():
         for k in range(3):
             wait(i_ref, ysend_sem.at[k])
 
-    @pl.when(owner)
-    def _():
-        for k in range(3, 6):
-            wait(i_ref, ysend_sem.at[k])
-
-    def sent(slot):
-        wait(r_ref, send_sem.at[slot])
-        wait(i_ref, send_sem.at[slot])
-
-    @pl.when(c == 0)
-    def _():
-        sent(2)
-
-    @pl.when(jnp.logical_and(c == 0, jnp.logical_or(z == 0, jnp.logical_or(z == 2, z == 6))))
-    def _():
-        sent(0)
-        sent(1)
-
-    @pl.when(jnp.logical_and(c == 0, jnp.logical_or(z == 3, z == 5)))
-    def _():
-        wait(r_ref.at[:, pl.ds(0, NB // 2), :], send_sem.at[0])
-        wait(i_ref.at[pl.ds(0, NB // 2), :], send_sem.at[0])
+    wide = jnp.logical_or(z == 0, jnp.logical_or(z == 2, z == 6))
+    half = jnp.logical_or(z == 3, z == 5)
+
+    @pl.when(first)
+    def _():
+        wait(r_ref, send_sem.at[2])
+
+        @pl.when(wide)
+        def _():
+            wait(r_ref, send_sem.at[0])
+            wait(r_ref, send_sem.at[1])
+
+        @pl.when(half)
+        def _():
+            wait(r_ref.at[:, pl.ds(0, NB // 2), :], send_sem.at[0])
+
+    @pl.when(second)
+    def _():
+        @pl.when(jnp.logical_not(beside_owner))
+        def _():
+            wait(i_ref, send_sem.at[2])
+
+        @pl.when(wide)
+        def _():
+            wait(i_ref, send_sem.at[0])
+            wait(i_ref, send_sem.at[1])
+
+        @pl.when(half)
+        def _():
+            wait(i_ref.at[pl.ds(0, NB // 2), :], send_sem.at[0])
 
 
 def gather(matrix):
@@ -343,7 +375,7 @@
         out_specs=[pl.BlockSpec(memory_space=pl.ANY)] * 3,
         scratch_shapes=[
             pltpu.VMEM((NB, NB), jnp.float32), pltpu.VMEM((NB, NB), jnp.float32), pltpu.VMEM((NB, NB), jnp.float32),
-            dma((T,)), dma((3,)), dma((6,)), dma((2,)), dma((T * PER,)), dma((4,)), dma((T,)), dma((T,)),
+            dma((T,)), dma((3,)), dma((7,)), dma((3,)), dma((T * PER,)), dma((4,)), dma((T,)), dma((T,)), dma((T,)),
         ],
         compiler_params=pltpu.CompilerParams(collective_id=0, has_side_effects=True, vmem_limit_bytes=50 * 2**20),
         name="gather",

time: 56 us -> 49.4 us (0.88)
  Pallas kernels: 55.5 us -> 49.2 us
    pallas_call x1, Pallas kernels: 50.8 us -> 44.4 us  [gather(): pl.pallas_call(gather_kernel, out_shape=(tiles, tiles, square), in_specs=...]
where the time goes in v3:
time: 49.4 us
  Pallas kernels  49.2 us (100%)
    pallas_call x1, Pallas kernels, gather(): pl.pallas_call(gather_kernel, out_shape=(tiles, tiles, square), in_specs=...  44.4 us
    pallas_call x1, Pallas kernels, update(): pl.pallas_call(update_kernel, out_shape=jax.ShapeDtypeStruct(flat, jnp.fl...  4.74 us

profile of v3, /device:TPU:128, one launch (start us, length us, event | category | flops | bytes accessed | tf_op | source)
XLA Modules:
  0.0 49.4 jit_solution(15575222955981215916)
XLA Ops:
  0.0 0.0 copy-start
  0.0 44.4 %gather.1 = (f32[5,256,256]{2,1,0:T(8,128)S(1)}, f32[5,256,256]{2,1,0:T(8,128)S(1)}, f32[256,256]{1,0:T(8,128)S(1)}) custom-call(f32[5,1,256,5,1,256]{5,4,3,2,1,0:T(1,128)} %a_ref.1), custom_call_target="tpu_custom_call" | custom-call | tf_op jit(solution)/shard_map/gather/pallas_call | solution.py:371
  44.5 0.0 copy-done
  44.5 4.7 %update.1 = f32[12800,128]{1,0:T(8,128)} custom-call(f32[12800,128]{1,0:T(8,128)S(1)} %bitcast.2, f32[5,256,256]{2,1,0:T(8,128)S(1)} %get-tuple-element.8.r_ref, f32[5,256,256]{2,1,0:T(8,128)S(1)} %get-tuple-element.9.c_ref, f32[256,256]{1,0:T(8,128)S(1)} %get-tuple-element.10.i_ref), custom_call_target="tpu_custom_call" | custom-call | tf_op jit(solution)/shard_map/update/pallas_call | solution.py:456
Async XLA Ops:
  0.0 44.5 %copy-start = (f32[5,1,256,5,1,256]{5,4,3,2,1,0:T(1,128)S(1)}, f32[5,1,256,5,1,256]{5,4,3,2,1,0:T(1,128)}, u32[]{:S(2)}) copy-start(f32[5,1,256,5,1,256]{5,4,3,2,1,0:T(1,128)} %a_ref.1) | copy-start | bytes 19660804

commit v4 on v3

--- a/solution.py
+++ b/solution.py
@@ -195,15 +195,24 @@
 
     mine = pl.ds(pl.multiple_of(p * SL, SL), SL)
 
+    def scatter_part(t, j):
+        for i in range(PER):
+            row = PER * j + i
+            part = pl.ds(row * SL, SL)
+
+            @pl.when(p != row)
+            def _(row=row, part=part):
+                pltpu.make_async_remote_copy(
+                    src_ref=r_ref.at[t, part, :], dst_ref=c_ref.at[t, part, :], send_sem=csend_sem.at[0],
+                    recv_sem=s_sem.at[t], device_id=(row, q), device_id_type=MESH).start()
+
+            @pl.when(p == row)
+            def _(part=part):
+                pltpu.make_async_copy(r_ref.at[t, part, :], c_ref.at[t, part, :], s_sem.at[t]).start()
+
     def scatter(t):
-        @pl.loop(1, 16)
-        def _(d):
-            row = lax.rem(p + d, 16)
-            part = pl.ds(pl.multiple_of(row * SL, SL), SL)
-            pltpu.make_async_remote_copy(
-                src_ref=r_ref.at[t, part, :], dst_ref=c_ref.at[t, part, :], send_sem=csend_sem.at[0],
-                recv_sem=s_sem.at[t], device_id=(row, q), device_id_type=MESH).start()
-        pltpu.make_async_copy(r_ref.at[t, mine, :], c_ref.at[t, mine, :], s_sem.at[t]).start()
+        for j in range(PER):
+            scatter_part(t, j)
 
     def share(t):
         wait(c_ref.at[t, mine, :], s_sem.at[t])
@@ -292,9 +301,9 @@
                 pass_z(r_chunk(n), r_sem.at[n], n)
                 remote(r_chunk(n), send_sem.at[2], r_sem.at[n], p, q + 1).start()
 
-        @pl.when(lead)
-        def _():
-            scatter(t)
+            @pl.when(lead)
+            def _(n=n):
+                scatter_part(t, n % PER)
 
     @pl.when(q != 0)
     def _():

time: 49.4 us -> 48.1 us (0.974)
  Pallas kernels: 49.2 us -> 47.9 us
    pallas_call x1, Pallas kernels: 44.4 us -> 43.1 us  [gather(): pl.pallas_call(gather_kernel, out_shape=(tiles, tiles, square), in_specs=...]
where the time goes in v4:
time: 48.1 us
  Pallas kernels  47.9 us (100%)
    pallas_call x1, Pallas kernels, gather(): pl.pallas_call(gather_kernel, out_shape=(tiles, tiles, square), in_specs=...  43.1 us
    pallas_call x1, Pallas kernels, update(): pl.pallas_call(update_kernel, out_shape=jax.ShapeDtypeStruct(flat, jnp.fl...  4.73 us

profile of v4, /device:TPU:128, one launch (start us, length us, event | category | flops | bytes accessed | tf_op | source)
XLA Modules:
  0.0 48.1 jit_solution(5432236607828994725)
XLA Ops:
  0.0 0.0 copy-start
  0.0 43.1 %gather.1 = (f32[5,256,256]{2,1,0:T(8,128)S(1)}, f32[5,256,256]{2,1,0:T(8,128)S(1)}, f32[256,256]{1,0:T(8,128)S(1)}) custom-call(f32[5,1,256,5,1,256]{5,4,3,2,1,0:T(1,128)} %a_ref.1), custom_call_target="tpu_custom_call" | custom-call | tf_op jit(solution)/shard_map/gather/pallas_call | solution.py:380
  43.2 0.0 copy-done
  43.2 4.7 %update.1 = f32[12800,128]{1,0:T(8,128)} custom-call(f32[12800,128]{1,0:T(8,128)S(1)} %bitcast.2, f32[5,256,256]{2,1,0:T(8,128)S(1)} %get-tuple-element.8.r_ref, f32[5,256,256]{2,1,0:T(8,128)S(1)} %get-tuple-element.9.c_ref, f32[256,256]{1,0:T(8,128)S(1)} %get-tuple-element.10.i_ref), custom_call_target="tpu_custom_call" | custom-call | tf_op jit(solution)/shard_map/update/pallas_call | solution.py:465
Async XLA Ops:
  0.0 43.2 %copy-start = (f32[5,1,256,5,1,256]{5,4,3,2,1,0:T(1,128)S(1)}, f32[5,1,256,5,1,256]{5,4,3,2,1,0:T(1,128)}, u32[]{:S(2)}) copy-start(f32[5,1,256,5,1,256]{5,4,3,2,1,0:T(1,128)} %a_ref.1) | copy-start | bytes 19660804

commit v5 on v4

--- a/solution.py
+++ b/solution.py
@@ -98,7 +98,7 @@
 
 
 ORDER = (1, 2, 3, 4, 0)
-STEPS = (("r", 0), ("r", 1), ("s", 0), ("r", 2), ("s", 1), ("y", 0), ("r", 3), ("s", 2), ("y", 1), ("r", 4), ("s", 3), ("y", 2), ("s", 4), ("y", 3), ("y", 4), ("i", 0), ("i", 1), ("i", 2), ("i", 3))
+STEPS = (("r", 0), ("s", 0), ("r", 1), ("s", 1), ("y", 0), ("r", 2), ("s", 2), ("y", 1), ("r", 3), ("s", 3), ("y", 2), ("r", 4), ("s", 4), ("y", 3), ("y", 4), ("i", 0), ("i", 1), ("i", 2), ("i", 3))
 
 
 def gather_kernel(a_ref, r_ref, c_ref, i_ref, a_v, w_ref, inv_v, load_sem, send_sem, ysend_sem, csend_sem, r_sem, i_sem, s_sem, x_sem, g_sem):

time: 48.1 us -> 53.3 us (1.11)
  Pallas kernels: 47.9 us -> 53.1 us
    pallas_call x1, Pallas kernels: 43.1 us -> 48.3 us  [gather(): pl.pallas_call(gather_kernel, out_shape=(tiles, tiles, square), in_specs=...]
where the time goes in v5:
time: 53.3 us
  Pallas kernels  53.1 us (100%)
    pallas_call x1, Pallas kernels, gather(): pl.pallas_call(gather_kernel, out_shape=(tiles, tiles, square), in_specs=...  48.3 us
    pallas_call x1, Pallas kernels, update(): pl.pallas_call(update_kernel, out_shape=jax.ShapeDtypeStruct(flat, jnp.fl...  4.74 us

profile of v5, /device:TPU:128, one launch (start us, length us, event | category | flops | bytes accessed | tf_op | source)
XLA Modules:
  0.0 53.3 jit_solution(687070054519202306)
XLA Ops:
  0.0 0.0 copy-start
  0.0 48.3 %gather.1 = (f32[5,256,256]{2,1,0:T(8,128)S(1)}, f32[5,256,256]{2,1,0:T(8,128)S(1)}, f32[256,256]{1,0:T(8,128)S(1)}) custom-call(f32[5,1,256,5,1,256]{5,4,3,2,1,0:T(1,128)} %a_ref.1), custom_call_target="tpu_custom_call" | custom-call | tf_op jit(solution)/shard_map/gather/pallas_call | solution.py:380
  48.4 0.0 copy-done
  48.4 4.7 %update.1 = f32[12800,128]{1,0:T(8,128)} custom-call(f32[12800,128]{1,0:T(8,128)S(1)} %bitcast.2, f32[5,256,256]{2,1,0:T(8,128)S(1)} %get-tuple-element.8.r_ref, f32[5,256,256]{2,1,0:T(8,128)S(1)} %get-tuple-element.9.c_ref, f32[256,256]{1,0:T(8,128)S(1)} %get-tuple-element.10.i_ref), custom_call_target="tpu_custom_call" | custom-call | tf_op jit(solution)/shard_map/update/pallas_call | solution.py:465
Async XLA Ops:
  0.0 48.4 %copy-start = (f32[5,1,256,5,1,256]{5,4,3,2,1,0:T(1,128)S(1)}, f32[5,1,256,5,1,256]{5,4,3,2,1,0:T(1,128)}, u32[]{:S(2)}) copy-start(f32[5,1,256,5,1,256]{5,4,3,2,1,0:T(1,128)} %a_ref.1) | copy-start | bytes 19660804
